TPU v7x, 32 devices: a whole 2x2x4 slice. The times are simulated.
32 devices in a mesh: node: 8 (over y, x, core), local: 4 (over z).
Axes of the slice: x: 2, y: 2, z: 4, core: 2. Of those that a mesh axis runs over, the one named last changes fastest.
Arguments:
- grad_out: bfloat16 [4096, 32, 384], P(('node', 'local')), may hold values from -6 to 6
- pooled: bfloat16 [4096, 32, 256], P(('node', 'local')), may hold values from -6 to 6
- proj: bfloat16 [32, 256, 128], P(('node', 'local')), may hold values from -0.5 to 0.5
- assign: int32 [32], replicated, may hold values from 0 to 31, each once
- indices: int32 [32, 4096, 3, 8], P(('node', 'local')), may hold values from 0 to 511
- lengths: int32 [32, 4096, 3], P(('node', 'local')), may hold values from 1 to 8
Outputs:
- table_grad: float32 [32, 512, 256], P(('node', 'local'))
- proj_grad: float32 [32, 256, 128], P(('node', 'local'))
Inputs may be any that keep to these rules, and one draw needn't show every extreme that they name: assign holds every group id once.
All inputs are finite; a program needn't handle non-finite values.
Results may differ from a plain program's by a relative error of at most 0.0029.
Values may be sent and summed in bfloat16 or wider, within the bound.
No kernel may reach another device: no remote copies, remote signals or barrier semaphores. Data moves between devices by JAX's collectives and lax.ppermute only.
A program may use at most 192 MiB of HBM per device.

v0:
```python
import functools
import math

import jax
import jax.numpy as jnp
from jax import lax
from jax.experimental import pallas as pl
from jax.experimental.pallas import tpu as pltpu
from jax.sharding import PartitionSpec as P

ROWS = 512
W1 = 16
W2 = 48
W3 = 192
PD = 128
W12 = W1 + W2
WSUM = W12 + W3
AXES = ("node", "local")
EB = 8
STEP = 32
MIB = 1024 * 1024


def params(grid):
    return pltpu.CompilerParams(dimension_semantics=("arbitrary",) * grid, vmem_limit_bytes=58 * MIB)


ANY = pl.BlockSpec(memory_space=pl.ANY)


def cost(flops):
    return pl.CostEstimate(flops=int(flops), bytes_accessed=1024, transcendentals=0)


def permute_kernel(slots, pieces, assign_ref, grad_ref, pool_ref, *refs):
    outs, (perm_ref, grad_held, pool_held, sems) = refs[:3], refs[3:]
    step = pl.program_id(0)
    sources = ((grad_ref, grad_held), (pool_ref, pool_held))

    def copies(i):
        at = pl.ds(i * STEP, STEP)
        return [
            pltpu.make_async_copy(ref.at[at], held.at[at], sems.at[n, i]) for n, (ref, held) in enumerate(sources)
        ]

    @pl.when(step == 0)
    def _():
        for i in range(grad_ref.shape[0] // STEP):
            for copy in copies(i):
                copy.start()
        width = EB * slots
        lane = lax.broadcasted_iota(jnp.int32, (2 * EB, width), 1)
        row = lax.broadcasted_iota(jnp.int32, (2 * EB, width), 0)
        for s in range(0, slots, 2):
            group = jnp.where(row < EB, assign_ref[s], assign_ref[s + 1])
            hit = lane == (row % EB) * slots + group
            perm_ref[s * EB : (s + 2) * EB, :] = jnp.where(hit, 1.0, 0.0).astype(jnp.bfloat16)

    for copy, (_, held), cuts in zip(copies(step), sources, pieces):
        copy.wait()
        width = held.shape[2]
        for start in range(0, STEP, 2 * EB):
            pair = []
            for at in (start, start + EB):
                block = held[pl.ds(step * STEP + at, EB)].reshape(EB * slots, width)
                moved = jnp.dot(perm_ref[...], block, preferred_element_type=jnp.float32)
                pair.append(moved.reshape(slots, EB, width))
            both = jnp.concatenate(pair, axis=1).astype(jnp.bfloat16)
            for n, low, high in cuts:
                outs[n][:, start : start + 2 * EB, :] = both[:, :, low:high]


def permute(assign, grad_out, pooled):
    count, slots, _ = grad_out.shape
    widths = (2 * PD, PD, WSUM)
    pieces = (((0, 0, 2 * PD), (1, 2 * PD, 3 * PD)), ((2, 0, WSUM),))
    return pl.pallas_call(
        functools.partial(permute_kernel, slots, pieces),
        out_shape=[jax.ShapeDtypeStruct((slots, count, width), jnp.bfloat16) for width in widths],
        grid_spec=pltpu.PrefetchScalarGridSpec(
            num_scalar_prefetch=1,
            grid=(count // STEP,),
            in_specs=[pl.BlockSpec(memory_space=pltpu.HBM)] * 2,
            out_specs=[pl.BlockSpec((slots, STEP, width), lambda i, a: (0, i, 0)) for width in widths],
            scratch_shapes=[
                pltpu.VMEM((EB * slots, EB * slots), jnp.bfloat16),
                pltpu.VMEM(grad_out.shape, jnp.bfloat16),
                pltpu.VMEM(pooled.shape, jnp.bfloat16),
                pltpu.SemaphoreType.DMA((2, count // STEP)),
            ],
        ),
        compiler_params=params(1),
        cost_estimate=cost(1e9),
        name="permute_groups",
    )(assign, grad_out, pooled)


def narrow_kernel(place_ref, g_ref, w_ref, out_ref):
    step, count, _ = g_ref.shape
    half = count // 2
    column = lax.broadcasted_iota(jnp.int32, (count, W12), 1)
    dims = (((1,), (1,)), ((), ()))
    for s in range(step):
        w = w_ref[place_ref[pl.program_id(0) * step + s]]
        first = lax.dot_general(g_ref[s, :, :PD], w, dims, preferred_element_type=jnp.float32)
        second = lax.dot_general(g_ref[s, :, PD:], w, dims, preferred_element_type=jnp.float32)
        d = jnp.where(column < W1, first, second)
        out_ref[s] = jnp.concatenate([d[:half], d[half:]], axis=1).astype(jnp.bfloat16)


def narrow_dpool(place, g12, w12):
    slots, count, _ = g12.shape
    step = 8
    return pl.pallas_call(
        narrow_kernel,
        out_shape=jax.ShapeDtypeStruct((slots, count // 2, 2 * W12), jnp.bfloat16),
        grid_spec=pltpu.PrefetchScalarGridSpec(
            num_scalar_prefetch=1,
            grid=(slots // step,),
            in_specs=[
                pl.BlockSpec((step, count, 2 * PD), lambda i, o: (i, 0, 0)),
                pl.BlockSpec((slots, W12, PD), lambda i, o: (0, 0, 0)),
            ],
            out_specs=pl.BlockSpec((step, count // 2, 2 * W12), lambda i, o: (i, 0, 0)),
        ),
        compiler_params=params(1),
        cost_estimate=cost(1e9),
        name="narrow_dpool",
    )(place, g12, w12)


def partial_kernel(chunks, add, node_ref, line_ref, q_ref, g12_ref, g3_ref, *refs):
    outs = refs[len(refs) - chunks :]
    size = outs[0].shape[0]

    def fill(out):
        for i in range(size):
            slot = line_ref[i]
            q = q_ref[slot].T
            narrow = jnp.dot(q[:W12], g12_ref[slot], preferred_element_type=jnp.float32)
            wide = jnp.dot(q[W12:], g3_ref[slot], preferred_element_type=jnp.float32)
            pieces = ((0, W1, narrow[:W1, :PD]), (W1, W12, narrow[W1:, PD:]), (W12, WSUM, wide))
            for start, end, piece in pieces:
                if add:
                    piece = piece + refs[0][i, start:end]
                out[i, start:end] = piece.astype(out.dtype)

    if chunks == 1:
        fill(outs[0])
    else:
        for c in range(chunks):
            pl.when(pl.program_id(0) == c)(functools.partial(fill, outs[c]))


def partial_proj(nodes, lines, q, g12, g3, other=None, after=()):
    slots, count, _ = q.shape
    chunks, size = nodes.shape[0], lines.shape[0]
    block = pl.BlockSpec((size, WSUM, PD), lambda i, n, o: (i, 0, 0))
    if other is None:
        added, outs, out_specs = (), 1, [block]
        out_shape = [jax.ShapeDtypeStruct((chunks * size, WSUM, PD), jnp.float32)]
    else:
        added, outs = (other,), chunks
        out_specs = [pl.BlockSpec((size, WSUM, PD), lambda i, n, o: (0, 0, 0))] * chunks
        out_shape = [
            jax.ShapeDtypeStruct((size, WSUM, PD), jnp.bfloat16 if c else jnp.float32) for c in range(chunks)
        ]
    return pl.pallas_call(
        functools.partial(partial_kernel, outs, other is not None),
        out_shape=out_shape,
        grid_spec=pltpu.PrefetchScalarGridSpec(
            num_scalar_prefetch=2,
            grid=(chunks,),
            in_specs=[
                pl.BlockSpec((size, count, width), lambda i, n, o: (n[i], 0, 0)) for width in (WSUM, 2 * PD, PD)
            ]
            + [block] * len(added)
            + [ANY] * len(after),
            out_specs=out_specs,
        ),
        compiler_params=params(1),
        cost_estimate=cost(1e9),
        name="partial_proj",
    )(nodes, lines, q, g12, g3, *added, *after)


def count_kernel(index_ref, length_ref, *refs):
    out_ref = refs[-1]
    bag, block = index_ref.shape[1], index_ref.shape[2]
    lanes, chunk, low = 256, 16, ROWS // 8

    def one(i, carry):
        at = pl.ds(pl.multiple_of(i * lanes, lanes), lanes)
        index = index_ref[0, :, at]
        which = lax.broadcasted_iota(jnp.int32, (bag, lanes), 0)
        key = jnp.where(which < length_ref[0, :, at], index & (low - 1), -1)
        unit = jnp.left_shift(jnp.int32(1), jnp.right_shift(index, 6) * 4)
        ids = lax.broadcasted_iota(jnp.int32, (chunk, lanes), 0)
        for c in range(low // chunk):
            total = jnp.zeros((chunk, lanes), jnp.int32)
            for j in range(bag):
                total = total + jnp.where(key[j : j + 1] == ids + c * chunk, unit[j : j + 1], 0)
            out_ref[0, c * chunk : (c + 1) * chunk, at] = total
        return carry

    lax.fori_loop(0, block // lanes, one, 0)


def count_hits(lookups, counts, after=()):
    tables, bag, examples = lookups.shape
    block = 2048
    return pl.pallas_call(
        count_kernel,
        out_shape=jax.ShapeDtypeStruct((tables, ROWS // 8, examples), jnp.int32),
        grid=(tables, examples // block),
        in_specs=[
            pl.BlockSpec((1, bag, block), lambda k, i: (k, 0, i)),
            pl.BlockSpec((1, 1, block), lambda k, i: (k, 0, i)),
        ]
        + [ANY] * len(after),
        out_specs=pl.BlockSpec((1, ROWS // 8, block), lambda k, i: (k, 0, i)),
        compiler_params=params(2),
        cost_estimate=cost(1e9),
        name="count_hits",
    )(lookups, counts, *after)


def unpacked(words):
    rows = [lax.shift_right_logical(words, jnp.int32(4 * n)) & 15 for n in range(8)]
    return jnp.concatenate([r.astype(jnp.float32).astype(jnp.bfloat16) for r in rows], axis=0)


def wide_kernel(hits_ref, g_ref, w_ref, out_ref):
    @pl.when(pl.program_id(0) == 0)
    def _():
        out_ref[...] = jnp.zeros_like(out_ref)

    block = g_ref.shape[0]
    column = lax.broadcasted_iota(jnp.int32, (block, WSUM), 1)
    d = lax.dot_general(g_ref[...], w_ref[...], (((1,), (1,)), ((), ())), preferred_element_type=jnp.float32)
    d = jnp.where(column < W12, 0.0, d).astype(jnp.bfloat16)
    out_ref[...] += jnp.dot(unpacked(hits_ref[0]), d, preferred_element_type=jnp.float32)


def wide_sum(hits, g3, weights):
    _, words, examples = hits.shape
    block = 1024
    return pl.pallas_call(
        wide_kernel,
        out_shape=jax.ShapeDtypeStruct((ROWS, WSUM), jnp.float32),
        grid=(examples // block,),
        in_specs=[
            pl.BlockSpec((1, words, block), lambda i: (2, 0, i)),
            pl.BlockSpec((block, PD), lambda i: (i, 0)),
            pl.BlockSpec((WSUM, PD), lambda i: (0, 0)),
        ],
        out_specs=pl.BlockSpec((ROWS, WSUM), lambda i: (0, 0)),
        compiler_params=params(1),
        cost_estimate=cost(1e9),
        name="wide_sum",
    )(hits, g3, weights)


def narrow_sum_kernel(hits_ref, d_ref, wide_ref, out_ref):
    @pl.when(pl.program_id(0) == 0)
    def _():
        out_ref[...] = wide_ref[...]

    sources = d_ref.shape[0]
    block = hits_ref.shape[2]
    column = lax.broadcasted_iota(jnp.int32, (block, PD), 1)
    pieces = []
    for d in range(sources):
        packed = d_ref[d].astype(jnp.float32)
        pieces += [packed, pltpu.roll(packed, PD - W12, 1)]
    both = jnp.concatenate(pieces, axis=0)
    d1 = jnp.where(column < W1, both, 0.0).astype(jnp.bfloat16)
    d2 = jnp.where((column >= W1) & (column < W12), both, 0.0).astype(jnp.bfloat16)
    out_ref[...] += jnp.dot(unpacked(hits_ref[0]), d1, preferred_element_type=jnp.float32) + jnp.dot(
        unpacked(hits_ref[1]), d2, preferred_element_type=jnp.float32
    )


def narrow_sum(hits, narrow, wide):
    _, words, examples = hits.shape
    sources, half, _ = narrow.shape
    block = 1024
    per = block // (2 * half)
    return pl.pallas_call(
        narrow_sum_kernel,
        out_shape=jax.ShapeDtypeStruct((ROWS, WSUM), jnp.float32),
        grid=(examples // block,),
        in_specs=[
            pl.BlockSpec((2, words, block), lambda i: (0, 0, i)),
            pl.BlockSpec((per, half, 2 * W12), lambda i: (i, 0, 0)),
            pl.BlockSpec((ROWS, PD), lambda i: (0, 0)),
        ],
        out_specs=pl.BlockSpec((ROWS, PD), lambda i: (0, 0)),
        input_output_aliases={2: 0},
        compiler_params=params(1),
        cost_estimate=cost(1e9),
        name="narrow_sum",
    )(hits, narrow, wide)


def swap(x, axis, size, bits):
    return lax.ppermute(x, axis, [(d, d ^ bits) for d in range(size)])


def local(sizes, grad_out, pooled, proj, assign, indices, lengths):
    count, slots, _ = grad_out.shape
    scale = 1.0 / math.sqrt(count * slots)
    n_node, n_local = sizes["node"], sizes["local"]
    n_plane = n_node // 2
    node, loc = lax.axis_index("node"), lax.axis_index("local")

    rows = proj[:, :W12]
    rows = jnp.concatenate([rows] + [swap(rows, "local", n_local, d) for d in range(1, n_local)])

    g12, g3, q = permute(assign, grad_out, pooled)

    rows, g3 = lax.optimization_barrier((rows, g3))
    rows = jnp.concatenate([rows] + [swap(rows, "node", n_node, 2 * d) for d in range(1, n_plane)])
    g3_got = lax.all_to_all(g3, AXES, split_axis=0, concat_axis=0, tiled=True)

    plane = jnp.arange(n_plane, dtype=jnp.int32) ^ (node // 2)
    lines = jnp.arange(n_local, dtype=jnp.int32) ^ loc
    (sent,) = partial_proj(plane * 2 + 1 - node % 2, lines, q, g12, g3, after=[rows])
    got = swap(sent, "node", n_node, 1)

    rows = jnp.concatenate([rows, swap(rows, "node", n_node, 1)])
    slot = jnp.arange(slots, dtype=jnp.int32)
    slot_node = slot // n_local ^ node
    slot_place = slot_node % 2 * (slots // 2) + slot_node // 2 * n_local + (slot % n_local ^ loc)
    narrow = narrow_dpool(slot_place, g12, rows)

    kept = partial_proj(plane * 2 + node % 2, lines, q, g12, g3, got, after=[narrow])
    arrived = [swap(kept[d], "node", n_node, 2 * d) for d in range(1, n_plane)]
    hits = count_hits(indices[0].transpose(1, 2, 0), lengths[0].T[:, None, :], after=kept[:1])

    narrow_sent, g3_got = lax.optimization_barrier((narrow, g3_got))
    narrow_got = lax.all_to_all(narrow_sent, AXES, split_axis=0, concat_axis=0, tiled=True)
    wide = wide_sum(hits, g3_got.reshape(-1, PD), proj[0])

    arrived, wide = lax.optimization_barrier((arrived, wide))
    total = kept[0]
    for term in arrived:
        total = total + term.astype(jnp.float32)
    proj_grad = total[:1]
    for d in range(1, n_local):
        proj_grad = proj_grad + swap(total[d : d + 1], "local", n_local, d)
    proj_grad = proj_grad * scale

    table_grad = narrow_sum(hits, narrow_got, wide)[None]
    return (table_grad, proj_grad)


def solution(mesh):
    placed = (
        P(AXES, None, None),
        P(AXES, None, None),
        P(AXES, None, None),
        P(),
        P(AXES, None, None, None),
        P(AXES, None, None),
    )
    return jax.shard_map(
        functools.partial(local, dict(mesh.shape)),
        mesh=mesh,
        in_specs=placed,
        out_specs=(P(AXES, None, None), P(AXES, None, None)),
        check_vma=False,
    )
```

profile of v0, /device:TPU:0, one launch (start us, length us, event | category | flops | bytes accessed | tf_op | source)
XLA Modules:
  0.0 97.0 jit_solution(7784230300781081532)
XLA Ops:
  1.4 5.0 %collective-permute-start.2 = (bf16[1,64,128]{2,1,0:T(8,128)(2,1)S(1)}, bf16[1,64,128]{2,1,0:T(8,128)(2,1)S(1)}, u32[]{:S(2)}, u32[]{:S(2)}) collective-permute-start(bf16[1,64,128]{2,1,0:T(8,128)(2,1)S(1)} %slice.15), channel_id=1, source_target_pairs={{0,3},{1,2},{2,1},{3,0},{4,7},{5,6},{6,5},{7,4},{8,11},{9,10},{10,... | collective-permute-start | bytes 49160 | tf_op jit(solution)/shard_map/ppermute | solution.py:307
  8.1 6.5 %permute_groups.1 = (bf16[32,128,256]{2,1,0:T(8,128)(2,1)}, bf16[32,128,128]{2,1,0:T(8,128)(2,1)}, bf16[32,128,256]{2,1,0:T(8,128)(2,1)}) custom-call(s32[32]{0:T(128)} %assign_ref.1, bf16[128,32,384]{2,1,0:T(8,128)(2,1)} %grad_ref.1, bf16[128,32,256]{2,1,0:T(8,128)(2,1)} %pool_ref.1), custom_call_target="tpu_custom_call" | custom-call | flops 1000000000 | bytes 1024 | tf_op jit(solution)/shard_map/permute_groups/pallas_call | solution.py:77
  14.6 1.8 %collective-permute-start.3 = (bf16[4,64,128]{2,1,0:T(8,128)(2,1)S(1)}, bf16[4,64,128]{2,1,0:T(8,128)(2,1)S(1)}, u32[]{:S(2)}, u32[]{:S(2)}) collective-permute-start(bf16[4,64,128]{2,1,0:T(8,128)(2,1)S(1)} %pad_maximum_fusion), channel_id=1, source_target_pairs={{0,8},{4,12},{8,0},{12,4},{16,24},{20,28},{24,16},{28,20},{1,9},{5... | collective-permute-start | bytes 196616 | tf_op jit(solution)/shard_map/ppermute | solution.py:307
  16.4 1.5 %collective-permute-start.4 = (bf16[4,64,128]{2,1,0:T(8,128)(2,1)S(1)}, bf16[4,64,128]{2,1,0:T(8,128)(2,1)S(1)}, u32[]{:S(2)}, u32[]{:S(2)}) collective-permute-start(bf16[4,64,128]{2,1,0:T(8,128)(2,1)S(1)} %pad_maximum_fusion), channel_id=1, source_target_pairs={{0,16},{4,20},{8,24},{12,28},{16,0},{20,4},{24,8},{28,12},{1,17},{... | collective-permute-start | bytes 196616 | tf_op jit(solution)/shard_map/ppermute | solution.py:307
  18.2 0.8 collective-permute-done.3
  19.0 2.3 %collective-permute-done.4 = bf16[4,64,128]{2,1,0:T(8,128)(2,1)S(1)} collective-permute-done((bf16[4,64,128]{2,1,0:T(8,128)(2,1)S(1)}, bf16[4,64,128]{2,1,0:T(8,128)(2,1)S(1)}, u32[]{:S(2)}, u32[]{:S(2)}) %collective-permute-start.4) | collective-permute-done | bytes 65568 | tf_op jit(solution)/shard_map/ppermute | solution.py:307
  21.3 1.7 %collective-permute-done.5 = bf16[4,64,128]{2,1,0:T(8,128)(2,1)S(1)} collective-permute-done((bf16[4,64,128]{2,1,0:T(8,128)(2,1)S(1)}, bf16[4,64,128]{2,1,0:T(8,128)(2,1)S(1)}, u32[]{:S(2)}, u32[]{:S(2)}) %collective-permute-start.5) | collective-permute-done | bytes 65568 | tf_op jit(solution)/shard_map/ppermute | solution.py:307
  23.1 0.8 copy-done.7
  24.6 5.0 %partial_proj.2 = f32[16,256,128]{2,1,0:T(8,128)} custom-call(s32[4]{0:T(128)} %add_subtract_fusion.node_ref, s32[4]{0:T(128)} %iota_xor_fusion.line_ref, bf16[32,128,256]{2,1,0:T(8,128)(2,1)} %get-tuple-element.17.q_ref, bf16[32,128,256]{2,1,0:T(8,128)(2,1)} %get-tuple-element.18.g12_ref.g_ref, bf16[32,128,128]{2,1,0:T(8,128)(2,1)} %get-tuple-element.20.g3_ref, ...), custom_call_target="tpu_custom_call" | custom-call | flops 1000000000 | bytes 1024 | tf_op jit(solution)/shard_map/partial_proj/pallas_call | solution.py:168
  29.6 4.1 %all-to-all-start = ((bf16[32,128,128]{2,1,0:T(8,128)(2,1)}), bf16[32,128,128]{2,1,0:T(8,128)(2,1)S(1)}, u32[]{:S(2)}, u32[]{:S(2)}) async-start(bf16[32,128,128]{2,1,0:T(8,128)(2,1)} %get-tuple-element.20.g3_ref), calls=%async_computation | async-start | bytes 2097152 | tf_op jit(solution)/shard_map/all_to_all | solution.py:324
  36.0 5.0 %narrow_dpool.1.refs_1_ = bf16[32,64,128]{2,1,0:T(8,128)(2,1)} custom-call(s32[32]{0:T(128)} %fusion.4.place_ref, bf16[32,128,256]{2,1,0:T(8,128)(2,1)} %get-tuple-element.18.g12_ref.g_ref, bf16[32,64,128]{2,1,0:T(8,128)(2,1)} %constant_dynamic-update-slice_fusion.4.w_ref), custom_call_target="tpu_custom_call" | custom-call | flops 1000000000 | bytes 1024 | tf_op jit(solution)/shard_map/narrow_dpool/pallas_call | solution.py:114
  41.1 1.4 %copy-done.2 = f32[16,256,128]{2,1,0:T(8,128)} copy-done((f32[16,256,128]{2,1,0:T(8,128)}, f32[16,256,128]{2,1,0:T(8,128)S(1)}, u32[]{:S(2)}) %copy-start.2) | copy-done | bytes 2097176
  42.4 5.4 %partial_proj.3 = (f32[4,256,128]{2,1,0:T(8,128)}, bf16[4,256,128]{2,1,0:T(8,128)(2,1)}, bf16[4,256,128]{2,1,0:T(8,128)(2,1)}, bf16[4,256,128]{2,1,0:T(8,128)(2,1)}) custom-call(s32[4]{0:T(128)} %fusion.8.node_ref, s32[4]{0:T(128)} %iota_xor_fusion.line_ref, bf16[32,128,256]{2,1,0:T(8,128)(2,1)} %get-tuple-element.17.q_ref, ...), custom_call_target="tpu_custom_call" | custom-call | flops 1000000000 | bytes 1024 | tf_op jit(solution)/shard_map/partial_proj/pallas_call | solution.py:168
  47.8 1.8 %collective-permute-start.8 = (bf16[4,256,128]{2,1,0:T(8,128)(2,1)}, bf16[4,256,128]{2,1,0:T(8,128)(2,1)S(1)}, u32[]{:S(2)}, u32[]{:S(2)}) collective-permute-start(bf16[4,256,128]{2,1,0:T(8,128)(2,1)} %get-tuple-element.24), channel_id=1, source_target_pairs={{0,8},{4,12},{8,0},{12,4},{16,24},{20,28},{24,16},{28,20},{1,9},{5... | collective-permute-start | bytes 786440 | tf_op jit(solution)/shard_map/ppermute | solution.py:307
  49.6 1.5 %collective-permute-start.9 = (bf16[4,256,128]{2,1,0:T(8,128)(2,1)}, bf16[4,256,128]{2,1,0:T(8,128)(2,1)S(1)}, u32[]{:S(2)}, u32[]{:S(2)}) collective-permute-start(bf16[4,256,128]{2,1,0:T(8,128)(2,1)} %get-tuple-element.25), channel_id=1, source_target_pairs={{0,16},{4,20},{8,24},{12,28},{16,0},{20,4},{24,8},{28,12},{1,17},{... | collective-permute-start | bytes 786440 | tf_op jit(solution)/shard_map/ppermute | solution.py:307
  52.0 6.7 %all-to-all-done = bf16[32,128,128]{2,1,0:T(8,128)(2,1)S(1)} async-done(((bf16[32,128,128]{2,1,0:T(8,128)(2,1)}), bf16[32,128,128]{2,1,0:T(8,128)(2,1)S(1)}, u32[]{:S(2)}, u32[]{:S(2)}) %all-to-all-start) | async-done | bytes 1048608 | tf_op jit(solution)/shard_map/all_to_all | solution.py:324
  58.8 4.6 %all-to-all-start.1 = ((bf16[32,64,128]{2,1,0:T(8,128)(2,1)}), bf16[32,64,128]{2,1,0:T(8,128)(2,1)S(1)}, u32[]{:S(2)}, u32[]{:S(2)}) async-start(bf16[32,64,128]{2,1,0:T(8,128)(2,1)} %narrow_dpool.1.refs_1_), calls=%async_computation.1 | async-start | bytes 1048576 | tf_op jit(solution)/shard_map/all_to_all | solution.py:342
  63.3 5.8 %count_hits.1.hits_ref = s32[3,64,4096]{2,1,0:T(8,128)} custom-call(s32[3,8,4096]{2,1,0:T(8,128)} %bitcast.13, s32[3,1,4096]{2,1,0:T(1,128)} %broadcast_in_dim.6.length_ref, f32[4,256,128]{2,1,0:T(8,128)} %get-tuple-element.22.refs_0_), custom_call_target="tpu_custom_call" | custom-call | flops 1000000000 | bytes 1024 | tf_op jit(solution)/shard_map/count_hits/pallas_call | solution.py:212
  69.2 5.5 %wide_sum.1.wide_ref = f32[512,256]{1,0:T(8,128)} custom-call(s32[3,64,4096]{2,1,0:T(8,128)} %count_hits.1.hits_ref, bf16[4096,128]{1,0:T(8,128)(2,1)} %bitcast.11, bf16[256,128]{1,0:T(8,128)(2,1)} %bitcast.15), custom_call_target="tpu_custom_call" | custom-call | flops 1000000000 | bytes 1024 | tf_op jit(solution)/shard_map/wide_sum/pallas_call | solution.py:248
  74.8 3.7 %collective-permute-start.13 = (f32[1,256,128]{2,1,0:T(8,128)S(1)}, f32[1,256,128]{2,1,0:T(8,128)S(1)}, u32[]{:S(2)}, u32[]{:S(2)}) collective-permute-start(f32[1,256,128]{2,1,0:T(8,128)S(1)} %get-tuple-element.33), channel_id=1, source_target_pairs={{0,3},{1,2},{2,1},{3,0},{4,7},{5,6},{6,5},{7,4},{8,11},{9,10},{10,... | collective-permute-start | bytes 393224 | tf_op jit(solution)/shard_map/ppermute | solution.py:307
  79.3 3.8 %collective-permute-done.13 = f32[1,256,128]{2,1,0:T(8,128)S(1)} collective-permute-done((f32[1,256,128]{2,1,0:T(8,128)S(1)}, f32[1,256,128]{2,1,0:T(8,128)S(1)}, u32[]{:S(2)}, u32[]{:S(2)}) %collective-permute-start.13) | collective-permute-done | bytes 131104 | tf_op jit(solution)/shard_map/ppermute | solution.py:307
  83.1 7.0 %collective-permute-done.12 = f32[1,256,128]{2,1,0:T(8,128)S(1)} collective-permute-done((f32[1,256,128]{2,1,0:T(8,128)S(1)}, f32[1,256,128]{2,1,0:T(8,128)S(1)}, u32[]{:S(2)}, u32[]{:S(2)}) %collective-permute-start.12) | collective-permute-done | bytes 131104 | tf_op jit(solution)/shard_map/ppermute | solution.py:307
  90.8 0.8 copy-done.1
  91.6 5.4 %narrow_sum.1 = f32[512,256]{1,0:T(8,128)} custom-call(s32[3,64,4096]{2,1,0:T(8,128)} %count_hits.1.hits_ref, bf16[32,64,128]{2,1,0:T(8,128)(2,1)} %copy-done.1, f32[512,256]{1,0:T(8,128)} %wide_sum.1.wide_ref), custom_call_target="tpu_custom_call", output_to_operand_aliasing={{}: (2, {})} | custom-call | flops 1000000000 | bytes 1024 | tf_op jit(solution)/shard_map/narrow_sum/pallas_call | solution.py:289
  (47 shorter events, 8.4 us)
Async XLA Ops:
  1.4 13.2 %collective-permute-start.2 = (bf16[1,64,128]{2,1,0:T(8,128)(2,1)S(1)}, bf16[1,64,128]{2,1,0:T(8,128)(2,1)S(1)}, u32[]{:S(2)}, u32[]{:S(2)}) collective-permute-start(bf16[1,64,128]{2,1,0:T(8,128)(2,1)S(1)} %slice.15), channel_id=1, source_target_pairs={{0,3},{1,2},{2,1},{3,0},{4,7},{5,6},{6,5},{7,4},{8,11},{9,10},{10,... | collective-permute-start | bytes 49160 | tf_op jit(solution)/shard_map/ppermute | solution.py:307
  6.4 8.2 %collective-permute-start.1 = (bf16[1,64,128]{2,1,0:T(8,128)(2,1)S(1)}, bf16[1,64,128]{2,1,0:T(8,128)(2,1)S(1)}, u32[]{:S(2)}, u32[]{:S(2)}) collective-permute-start(bf16[1,64,128]{2,1,0:T(8,128)(2,1)S(1)} %slice.15), channel_id=1, source_target_pairs={{0,2},{1,3},{2,0},{3,1},{4,6},{5,7},{6,4},{7,5},{8,10},{9,11},{10,... | collective-permute-start | bytes 49160 | tf_op jit(solution)/shard_map/ppermute | solution.py:307
  6.4 8.2 %collective-permute-start = (bf16[1,64,128]{2,1,0:T(8,128)(2,1)S(1)}, bf16[1,64,128]{2,1,0:T(8,128)(2,1)S(1)}, u32[]{:S(2)}, u32[]{:S(2)}) collective-permute-start(bf16[1,64,128]{2,1,0:T(8,128)(2,1)S(1)} %slice.15), channel_id=1, source_target_pairs={{0,1},{1,0},{2,3},{3,2},{4,5},{5,4},{6,7},{7,6},{8,9},{9,8},{10,11... | collective-permute-start | bytes 49160 | tf_op jit(solution)/shard_map/ppermute | solution.py:307
  14.6 4.4 %collective-permute-start.3 = (bf16[4,64,128]{2,1,0:T(8,128)(2,1)S(1)}, bf16[4,64,128]{2,1,0:T(8,128)(2,1)S(1)}, u32[]{:S(2)}, u32[]{:S(2)}) collective-permute-start(bf16[4,64,128]{2,1,0:T(8,128)(2,1)S(1)} %pad_maximum_fusion), channel_id=1, source_target_pairs={{0,8},{4,12},{8,0},{12,4},{16,24},{20,28},{24,16},{28,20},{1,9},{5... | collective-permute-start | bytes 196616 | tf_op jit(solution)/shard_map/ppermute | solution.py:307
  16.4 4.9 %collective-permute-start.4 = (bf16[4,64,128]{2,1,0:T(8,128)(2,1)S(1)}, bf16[4,64,128]{2,1,0:T(8,128)(2,1)S(1)}, u32[]{:S(2)}, u32[]{:S(2)}) collective-permute-start(bf16[4,64,128]{2,1,0:T(8,128)(2,1)S(1)} %pad_maximum_fusion), channel_id=1, source_target_pairs={{0,16},{4,20},{8,24},{12,28},{16,0},{20,4},{24,8},{28,12},{1,17},{... | collective-permute-start | bytes 196616 | tf_op jit(solution)/shard_map/ppermute | solution.py:307
  17.9 5.2 %collective-permute-start.5 = (bf16[4,64,128]{2,1,0:T(8,128)(2,1)S(1)}, bf16[4,64,128]{2,1,0:T(8,128)(2,1)S(1)}, u32[]{:S(2)}, u32[]{:S(2)}) collective-permute-start(bf16[4,64,128]{2,1,0:T(8,128)(2,1)S(1)} %pad_maximum_fusion), channel_id=1, source_target_pairs={{0,24},{4,28},{8,16},{12,20},{16,8},{20,12},{24,0},{28,4},{1,25},{... | collective-permute-start | bytes 196616 | tf_op jit(solution)/shard_map/ppermute | solution.py:307
  23.1 0.8 copy-start.7
  23.9 0.7 copy-start.4
  29.6 4.1 %copy-start.5 = (bf16[16,64,128]{2,1,0:T(8,128)(2,1)S(1)}, bf16[16,64,128]{2,1,0:T(8,128)(2,1)}, u32[]{:S(2)}) copy-start(bf16[16,64,128]{2,1,0:T(8,128)(2,1)} %copy-done.4) | copy-start | bytes 786436
  29.6 11.4 %collective-permute-start.6 = (f32[16,256,128]{2,1,0:T(8,128)}, f32[16,256,128]{2,1,0:T(8,128)S(1)}, u32[]{:S(2)}, u32[]{:S(2)}) collective-permute-start(f32[16,256,128]{2,1,0:T(8,128)} %partial_proj.2), channel_id=1, source_target_pairs={{0,4},{4,0},{8,12},{12,8},{16,20},{20,16},{24,28},{28,24},{1,5},{5... | collective-permute-start | bytes 6291464 | tf_op jit(solution)/shard_map/ppermute | solution.py:307
  29.6 29.1 %all-to-all-start = ((bf16[32,128,128]{2,1,0:T(8,128)(2,1)}), bf16[32,128,128]{2,1,0:T(8,128)(2,1)S(1)}, u32[]{:S(2)}, u32[]{:S(2)}) async-start(bf16[32,128,128]{2,1,0:T(8,128)(2,1)} %get-tuple-element.20.g3_ref), calls=%async_computation | async-start | bytes 2097152 | tf_op jit(solution)/shard_map/all_to_all | solution.py:324
  33.7 1.6 %collective-permute-start.7 = (bf16[16,64,128]{2,1,0:T(8,128)(2,1)S(1)}, bf16[16,64,128]{2,1,0:T(8,128)(2,1)S(1)}, u32[]{:S(2)}, u32[]{:S(2)}) collective-permute-start(bf16[16,64,128]{2,1,0:T(8,128)(2,1)S(1)} %copy-done.5), channel_id=1, source_target_pairs={{0,4},{4,0},{8,12},{12,8},{16,20},{20,16},{24,28},{28,24},{1,5},{5... | collective-permute-start | bytes 786440 | tf_op jit(solution)/shard_map/ppermute | solution.py:307
  41.1 10.3 %copy-start.6 = (s32[1,4096,3]{1,0,2:T(1,128)S(1)}, s32[1,4096,3]{1,0,2:T(1,128)}, u32[]{:S(2)}) copy-start(s32[1,4096,3]{1,0,2:T(1,128)} %param.11) | copy-start | bytes 147460
  41.1 1.4 %copy-start.2 = (f32[16,256,128]{2,1,0:T(8,128)}, f32[16,256,128]{2,1,0:T(8,128)S(1)}, u32[]{:S(2)}) copy-start(f32[16,256,128]{2,1,0:T(8,128)S(1)} %collective-permute-done.6.refs_0_) | copy-start | bytes 6291460
  47.8 26.8 %collective-permute-start.8 = (bf16[4,256,128]{2,1,0:T(8,128)(2,1)}, bf16[4,256,128]{2,1,0:T(8,128)(2,1)S(1)}, u32[]{:S(2)}, u32[]{:S(2)}) collective-permute-start(bf16[4,256,128]{2,1,0:T(8,128)(2,1)} %get-tuple-element.24), channel_id=1, source_target_pairs={{0,8},{4,12},{8,0},{12,4},{16,24},{20,28},{24,16},{28,20},{1,9},{5... | collective-permute-start | bytes 786440 | tf_op jit(solution)/shard_map/ppermute | solution.py:307
  49.6 25.0 %collective-permute-start.9 = (bf16[4,256,128]{2,1,0:T(8,128)(2,1)}, bf16[4,256,128]{2,1,0:T(8,128)(2,1)S(1)}, u32[]{:S(2)}, u32[]{:S(2)}) collective-permute-start(bf16[4,256,128]{2,1,0:T(8,128)(2,1)} %get-tuple-element.25), channel_id=1, source_target_pairs={{0,16},{4,20},{8,24},{12,28},{16,0},{20,4},{24,8},{28,12},{1,17},{... | collective-permute-start | bytes 786440 | tf_op jit(solution)/shard_map/ppermute | solution.py:307
  51.1 23.6 %collective-permute-start.10 = (bf16[4,256,128]{2,1,0:T(8,128)(2,1)}, bf16[4,256,128]{2,1,0:T(8,128)(2,1)S(1)}, u32[]{:S(2)}, u32[]{:S(2)}) collective-permute-start(bf16[4,256,128]{2,1,0:T(8,128)(2,1)} %get-tuple-element.26), channel_id=1, source_target_pairs={{0,24},{4,28},{8,16},{12,20},{16,8},{20,12},{24,0},{28,4},{1,25},{... | collective-permute-start | bytes 786440 | tf_op jit(solution)/shard_map/ppermute | solution.py:307
  58.8 10.4 %copy-start = (bf16[32,128,128]{2,1,0:T(8,128)(2,1)}, bf16[32,128,128]{2,1,0:T(8,128)(2,1)S(1)}, u32[]{:S(2)}) copy-start(bf16[32,128,128]{2,1,0:T(8,128)(2,1)S(1)} %all-to-all-done) | copy-start | bytes 3145732
  58.8 32.0 %all-to-all-start.1 = ((bf16[32,64,128]{2,1,0:T(8,128)(2,1)}), bf16[32,64,128]{2,1,0:T(8,128)(2,1)S(1)}, u32[]{:S(2)}, u32[]{:S(2)}) async-start(bf16[32,64,128]{2,1,0:T(8,128)(2,1)} %narrow_dpool.1.refs_1_), calls=%async_computation.1 | async-start | bytes 1048576 | tf_op jit(solution)/shard_map/all_to_all | solution.py:342
  69.2 5.5 %copy-start.3 = (f32[4,256,128]{2,1,0:T(8,128)S(1)}, f32[4,256,128]{2,1,0:T(8,128)}, u32[]{:S(2)}) copy-start(f32[4,256,128]{2,1,0:T(8,128)} %get-tuple-element.22.refs_0_) | copy-start | bytes 1572868
  74.8 8.3 %collective-permute-start.13 = (f32[1,256,128]{2,1,0:T(8,128)S(1)}, f32[1,256,128]{2,1,0:T(8,128)S(1)}, u32[]{:S(2)}, u32[]{:S(2)}) collective-permute-start(f32[1,256,128]{2,1,0:T(8,128)S(1)} %get-tuple-element.33), channel_id=1, source_target_pairs={{0,3},{1,2},{2,1},{3,0},{4,7},{5,6},{6,5},{7,4},{8,11},{9,10},{10,... | collective-permute-start | bytes 393224 | tf_op jit(solution)/shard_map/ppermute | solution.py:307
  78.5 11.6 %collective-permute-start.12 = (f32[1,256,128]{2,1,0:T(8,128)S(1)}, f32[1,256,128]{2,1,0:T(8,128)S(1)}, u32[]{:S(2)}, u32[]{:S(2)}) collective-permute-start(f32[1,256,128]{2,1,0:T(8,128)S(1)} %get-tuple-element.34), channel_id=1, source_target_pairs={{0,2},{1,3},{2,0},{3,1},{4,6},{5,7},{6,4},{7,5},{8,10},{9,11},{10,... | collective-permute-start | bytes 393224 | tf_op jit(solution)/shard_map/ppermute | solution.py:307
  78.5 11.6 %collective-permute-start.11 = (f32[1,256,128]{2,1,0:T(8,128)S(1)}, f32[1,256,128]{2,1,0:T(8,128)S(1)}, u32[]{:S(2)}, u32[]{:S(2)}) collective-permute-start(f32[1,256,128]{2,1,0:T(8,128)S(1)} %get-tuple-element.32), channel_id=1, source_target_pairs={{0,1},{1,0},{2,3},{3,2},{4,5},{5,4},{6,7},{7,6},{8,9},{9,8},{10,11... | collective-permute-start | bytes 393224 | tf_op jit(solution)/shard_map/ppermute | solution.py:307
  90.8 0.8 copy-start.1
where the time goes:
time: 97.9 us; the launch traced here: 97 us
  Pallas kernels  38.6 us (39%)
  starting transfers between devices  26.1 us (27%)
  waiting for transfers between devices  22.6 us (23%)
  local copies, waits for them, and re-layouts  5.94 us (6%)
  other arithmetic  2.95 us (3%)
    ppermute x14, starting transfers between devices, swap(): return lax.ppermute(x, axis, [(d, d ^ bits) for d in range(size)])  17.4 us
    ppermute x14, waiting for transfers between devices, swap(): return lax.ppermute(x, axis, [(d, d ^ bits) for d in range(size)])  15.9 us
    pallas_call x2, Pallas kernels, partial_proj(): pl.pallas_call(functools.partial(partial_kernel, outs, other is not None)...  10.4 us
    all_to_all x1, waiting for transfers between devices, local(): g3_got = lax.all_to_all(g3, AXES, split_axis=0, concat_axis=0, tiled=True)  6.74 us
    pallas_call x1, Pallas kernels, permute(): pl.pallas_call(functools.partial(permute_kernel, slots, pieces), out_shap...  6.48 us
    pallas_call x1, Pallas kernels, count_hits(): pl.pallas_call(count_kernel, out_shape=jax.ShapeDtypeStruct((tables, ROWS...  5.82 us
    pallas_call x1, Pallas kernels, wide_sum(): pl.pallas_call(wide_kernel, out_shape=jax.ShapeDtypeStruct((ROWS, WSUM),...  5.47 us
    pallas_call x1, Pallas kernels, narrow_sum(): pl.pallas_call(narrow_sum_kernel, out_shape=jax.ShapeDtypeStruct((ROWS, W...  5.39 us
  transfers between devices with their start and end apart: 16, of which 7 were waited for; matrix products, arithmetic and copies ran while one was open for 5% of the time, Pallas kernels for 29%

commit v1 on v0

v1 whole, which is shorter than its diff:
```python
import functools
import math

import jax
import jax.numpy as jnp
from jax import lax
from jax.experimental import pallas as pl
from jax.experimental.pallas import tpu as pltpu
from jax.sharding import PartitionSpec as P

ROWS = 512
W1 = 16
W2 = 48
W3 = 192
PD = 128
W12 = W1 + W2
WSUM = W12 + W3
AXES = ("node", "local")
EB = 8
STEP = 16
MIB = 1024 * 1024


def params(grid):
    return pltpu.CompilerParams(dimension_semantics=("arbitrary",) * grid, vmem_limit_bytes=58 * MIB)


HBM = pl.BlockSpec(memory_space=pltpu.HBM)
ANY = pl.BlockSpec(memory_space=pl.ANY)


def cost(flops):
    return pl.CostEstimate(flops=int(flops), bytes_accessed=1024, transcendentals=0)


def permute_kernel(slots, pieces, assign_ref, grad_ref, pool_ref, *refs):
    outs, (perm_ref, grad_held, pool_held, sems) = refs[:3], refs[3:]
    step = pl.program_id(0)
    sources = ((grad_ref, grad_held), (pool_ref, pool_held))

    def copies(i):
        at = pl.ds(i * STEP, STEP)
        return [
            pltpu.make_async_copy(ref.at[at], held.at[at], sems.at[n, i]) for n, (ref, held) in enumerate(sources)
        ]

    @pl.when(step == 0)
    def _():
        for i in range(grad_ref.shape[0] // STEP):
            for copy in copies(i):
                copy.start()
        width = EB * slots
        lane = lax.broadcasted_iota(jnp.int32, (2 * EB, width), 1)
        row = lax.broadcasted_iota(jnp.int32, (2 * EB, width), 0)
        for s in range(0, slots, 2):
            group = jnp.where(row < EB, assign_ref[s], assign_ref[s + 1])
            hit = lane == (row % EB) * slots + group
            perm_ref[s * EB : (s + 2) * EB, :] = jnp.where(hit, 1.0, 0.0).astype(jnp.bfloat16)

    for copy, (_, held), cuts in zip(copies(step), sources, pieces):
        copy.wait()
        width = held.shape[2]
        for start in range(0, STEP, 2 * EB):
            pair = []
            for at in (start, start + EB):
                block = held[pl.ds(step * STEP + at, EB)].reshape(EB * slots, width)
                moved = jnp.dot(perm_ref[...], block, preferred_element_type=jnp.float32)
                pair.append(moved.reshape(slots, EB, width))
            both = jnp.concatenate(pair, axis=1).astype(jnp.bfloat16)
            for n, low, high in cuts:
                outs[n][:, start : start + 2 * EB, :] = both[:, :, low:high]


def permute(assign, grad_out, pooled):
    count, slots, _ = grad_out.shape
    widths = (2 * PD, PD, WSUM)
    pieces = (((0, 0, 2 * PD), (1, 2 * PD, 3 * PD)), ((2, 0, WSUM),))
    return pl.pallas_call(
        functools.partial(permute_kernel, slots, pieces),
        out_shape=[jax.ShapeDtypeStruct((slots, count, width), jnp.bfloat16) for width in widths],
        grid_spec=pltpu.PrefetchScalarGridSpec(
            num_scalar_prefetch=1,
            grid=(count // STEP,),
            in_specs=[HBM] * 2,
            out_specs=[pl.BlockSpec((slots, STEP, width), lambda i, a: (0, i, 0)) for width in widths],
            scratch_shapes=[
                pltpu.VMEM((EB * slots, EB * slots), jnp.bfloat16),
                pltpu.VMEM(grad_out.shape, jnp.bfloat16),
                pltpu.VMEM(pooled.shape, jnp.bfloat16),
                pltpu.SemaphoreType.DMA((2, count // STEP)),
            ],
        ),
        compiler_params=params(1),
        cost_estimate=cost(1e7),
        name="permute_groups",
    )(assign, grad_out, pooled)


def fetch(ref, held, sems, blocks, pick=lambda i: i):
    size = held.shape[0] // blocks
    copies = [
        pltpu.make_async_copy(ref.at[pl.ds(pick(i) * size, size)], held.at[pl.ds(i * size, size)], sems.at[i])
        for i in range(blocks)
    ]
    for copy in copies:
        copy.start()
    return copies


def narrow_kernel(blocks, place_ref, g_ref, w_ref, out_ref, g_held, w_held, out_held, g_sems, w_sems, out_sems):
    weights = fetch(w_ref, w_held, w_sems, 1)
    loads = fetch(g_ref, g_held, g_sems, blocks)
    slots, count, _ = g_held.shape
    step, half = slots // blocks, count // 2
    column = lax.broadcasted_iota(jnp.int32, (count, W12), 1)
    dims = (((1,), (1,)), ((), ()))
    weights[0].wait()
    stores = []
    for i, load in enumerate(loads):
        load.wait()
        for s in range(i * step, (i + 1) * step):
            w = w_held[place_ref[s]]
            first = lax.dot_general(g_held[s, :, :PD], w, dims, preferred_element_type=jnp.float32)
            second = lax.dot_general(g_held[s, :, PD:], w, dims, preferred_element_type=jnp.float32)
            d = jnp.where(column < W1, first, second)
            out_held[s] = jnp.concatenate([d[:half], d[half:]], axis=1).astype(jnp.bfloat16)
        at = pl.ds(i * step, step)
        stores.append(pltpu.make_async_copy(out_held.at[at], out_ref.at[at], out_sems.at[i]))
        stores[-1].start()
    for store in stores:
        store.wait()


def narrow_dpool(place, g12, w12):
    slots, count, _ = g12.shape
    blocks = 4
    shape = (slots, count // 2, 2 * W12)
    return pl.pallas_call(
        functools.partial(narrow_kernel, blocks),
        out_shape=jax.ShapeDtypeStruct(shape, jnp.bfloat16),
        grid_spec=pltpu.PrefetchScalarGridSpec(
            num_scalar_prefetch=1,
            grid=(1,),
            in_specs=[HBM] * 2,
            out_specs=HBM,
            scratch_shapes=[
                pltpu.VMEM(g12.shape, jnp.bfloat16),
                pltpu.VMEM(w12.shape, jnp.bfloat16),
                pltpu.VMEM(shape, jnp.bfloat16),
                pltpu.SemaphoreType.DMA((blocks,)),
                pltpu.SemaphoreType.DMA((1,)),
                pltpu.SemaphoreType.DMA((blocks,)),
            ],
        ),
        compiler_params=params(1),
        cost_estimate=cost(1e7),
        name="narrow_dpool",
    )(place, g12, w12)


def partial_kernel(ins, waits, outs, node_ref, line_ref, *refs):
    operands, results = refs[:ins], refs[ins + waits : ins + waits + outs]
    held, out_held = refs[-2 - ins - outs : -2 - outs], refs[-2 - outs : -2]
    in_sems, out_sems = refs[-2:]
    blocks, size = node_ref.shape[0], line_ref.shape[0]
    loads = [
        fetch(ref, at, in_sems.at[n], blocks, (lambda i: node_ref[i]) if n < 3 else (lambda i: i))
        for n, (ref, at) in enumerate(zip(operands, held))
    ]
    stores = []
    for i in range(blocks):
        for copies in loads:
            copies[i].wait()
        if outs == 1:
            at = pl.ds(i * size, size)
            result, out = results[0].at[at], out_held[0].at[at]
        else:
            result, out = results[i], out_held[i]
        for l in range(size):
            slot = i * size + line_ref[l]
            q = held[0][slot].T
            narrow = jnp.dot(q[:W12], held[1][slot], preferred_element_type=jnp.float32)
            wide = jnp.dot(q[W12:], held[2][slot], preferred_element_type=jnp.float32)
            pieces = ((0, W1, narrow[:W1, :PD]), (W1, W12, narrow[W1:, PD:]), (W12, WSUM, wide))
            for start, end, piece in pieces:
                if ins == 4:
                    piece = piece + held[3][i * size + l, start:end]
                out[l, start:end] = piece.astype(out.dtype)
        stores.append(pltpu.make_async_copy(out, result, out_sems.at[i]))
        stores[-1].start()
    for store in stores:
        store.wait()


def partial_proj(nodes, lines, q, g12, g3, other=None, after=()):
    _, count, _ = q.shape
    blocks, size = nodes.shape[0], lines.shape[0]
    every = (blocks * size, WSUM, PD)
    if other is None:
        added, shapes = (), [jax.ShapeDtypeStruct(every, jnp.float32)]
    else:
        kinds = [jnp.float32] + [jnp.bfloat16] * (blocks - 1)
        added, shapes = (other,), [jax.ShapeDtypeStruct((size, WSUM, PD), kind) for kind in kinds]
    ins = 3 + len(added)
    return pl.pallas_call(
        functools.partial(partial_kernel, ins, len(after), len(shapes)),
        out_shape=shapes,
        grid_spec=pltpu.PrefetchScalarGridSpec(
            num_scalar_prefetch=2,
            grid=(1,),
            in_specs=[HBM] * ins + [ANY] * len(after),
            out_specs=[HBM] * len(shapes),
            scratch_shapes=[pltpu.VMEM((blocks * size, count, x.shape[2]), jnp.bfloat16) for x in (q, g12, g3)]
            + [pltpu.VMEM(every, jnp.float32)] * len(added)
            + [pltpu.VMEM(x.shape, x.dtype) for x in shapes]
            + [pltpu.SemaphoreType.DMA((ins, blocks)), pltpu.SemaphoreType.DMA((blocks,))],
        ),
        compiler_params=params(1),
        cost_estimate=cost(1e7),
        name="partial_proj",
    )(nodes, lines, q, g12, g3, *added, *after)


def count_kernel(index_ref, length_ref, *refs):
    out_ref = refs[-1]
    bag, block = index_ref.shape[1], index_ref.shape[2]
    lanes, chunk, low = 256, 16, ROWS // 8

    def one(i, carry):
        at = pl.ds(pl.multiple_of(i * lanes, lanes), lanes)
        index = index_ref[0, :, at]
        which = lax.broadcasted_iota(jnp.int32, (bag, lanes), 0)
        key = jnp.where(which < length_ref[0, :, at], index & (low - 1), -1)
        unit = jnp.left_shift(jnp.int32(1), jnp.right_shift(index, 6) * 4)
        ids = lax.broadcasted_iota(jnp.int32, (chunk, lanes), 0)
        for c in range(low // chunk):
            total = jnp.zeros((chunk, lanes), jnp.int32)
            for j in range(bag):
                total = total + jnp.where(key[j : j + 1] == ids + c * chunk, unit[j : j + 1], 0)
            out_ref[0, c * chunk : (c + 1) * chunk, at] = total
        return carry

    lax.fori_loop(0, block // lanes, one, 0)


def count_hits(lookups, counts, after=()):
    tables, bag, examples = lookups.shape
    block = 4096
    return pl.pallas_call(
        count_kernel,
        out_shape=jax.ShapeDtypeStruct((tables, ROWS // 8, examples), jnp.int32),
        grid=(tables, examples // block),
        in_specs=[
            pl.BlockSpec((1, bag, block), lambda k, i: (k, 0, i)),
            pl.BlockSpec((1, 1, block), lambda k, i: (k, 0, i)),
        ]
        + [ANY] * len(after),
        out_specs=pl.BlockSpec((1, ROWS // 8, block), lambda k, i: (k, 0, i)),
        compiler_params=params(2),
        cost_estimate=cost(1e7),
        name="count_hits",
    )(lookups, counts, *after)


def unpacked(words):
    rows = [lax.shift_right_logical(words, jnp.int32(4 * n)) & 15 for n in range(8)]
    return jnp.concatenate([r.astype(jnp.float32).astype(jnp.bfloat16) for r in rows], axis=0)


def fetch_words(ref, held, sems, tables, blocks):
    size = ref.shape[2] // blocks
    copies = []
    for i in range(blocks):
        at = pl.ds(i * size, size)
        copies.append(
            [pltpu.make_async_copy(ref.at[k, :, at], held.at[n, :, at], sems.at[n, i]) for n, k in enumerate(tables)]
        )
        for copy in copies[-1]:
            copy.start()
    return copies


def wide_kernel(blocks, hits_ref, g_ref, w_ref, *refs):
    out_ref, hits_held, g_held, hits_sems, g_sems = refs[-5:]
    hits = fetch_words(hits_ref, hits_held, hits_sems, (2,), blocks)
    loads = fetch(g_ref, g_held, g_sems, blocks)
    block = g_held.shape[0] // blocks
    column = lax.broadcasted_iota(jnp.int32, (block, WSUM), 1)
    for i in range(blocks):
        at = slice(i * block, (i + 1) * block)
        loads[i].wait()
        d = lax.dot_general(g_held[at], w_ref[...], (((1,), (1,)), ((), ())), preferred_element_type=jnp.float32)
        d = jnp.where(column < W12, 0.0, d).astype(jnp.bfloat16)
        hits[i][0].wait()
        term = jnp.dot(unpacked(hits_held[0, :, at]), d, preferred_element_type=jnp.float32)
        out_ref[...] = term if i == 0 else out_ref[...] + term


def wide_sum(hits, g3, weights, after=()):
    _, words, examples = hits.shape
    blocks = 4
    return pl.pallas_call(
        functools.partial(wide_kernel, blocks),
        out_shape=jax.ShapeDtypeStruct((ROWS, WSUM), jnp.float32),
        in_specs=[HBM, HBM, pl.BlockSpec(memory_space=pltpu.VMEM)] + [ANY] * len(after),
        out_specs=pl.BlockSpec(memory_space=pltpu.VMEM),
        scratch_shapes=[
            pltpu.VMEM((1, words, examples), jnp.int32),
            pltpu.VMEM(g3.shape, jnp.bfloat16),
            pltpu.SemaphoreType.DMA((1, blocks)),
            pltpu.SemaphoreType.DMA((blocks,)),
        ],
        compiler_params=params(0),
        cost_estimate=cost(1e7),
        name="wide_sum",
    )(hits, g3, weights, *after)


def narrow_sum_kernel(blocks, hits_ref, d_ref, wide_ref, out_ref, hits_held, d_held, hits_sems, d_sems):
    hits = fetch_words(hits_ref, hits_held, hits_sems, (0, 1), blocks)
    loads = fetch(d_ref, d_held, d_sems, blocks)
    sources, block = d_held.shape[0] // blocks, hits_held.shape[2] // blocks
    column = lax.broadcasted_iota(jnp.int32, (block, PD), 1)
    out_ref[...] = wide_ref[...]
    for i in range(blocks):
        at = slice(i * block, (i + 1) * block)
        loads[i].wait()
        pieces = []
        for d in range(i * sources, (i + 1) * sources):
            packed = d_held[d].astype(jnp.float32)
            pieces += [packed, pltpu.roll(packed, PD - W12, 1)]
        both = jnp.concatenate(pieces, axis=0)
        d1 = jnp.where(column < W1, both, 0.0).astype(jnp.bfloat16)
        d2 = jnp.where((column >= W1) & (column < W12), both, 0.0).astype(jnp.bfloat16)
        for n, d in enumerate((d1, d2)):
            hits[i][n].wait()
            out_ref[...] += jnp.dot(unpacked(hits_held[n, :, at]), d, preferred_element_type=jnp.float32)


def narrow_sum(hits, narrow, wide):
    _, words, examples = hits.shape
    blocks = 4
    return pl.pallas_call(
        functools.partial(narrow_sum_kernel, blocks),
        out_shape=jax.ShapeDtypeStruct((ROWS, WSUM), jnp.float32),
        grid=(1,),
        in_specs=[HBM, HBM, pl.BlockSpec((ROWS, PD), lambda i: (0, 0))],
        out_specs=pl.BlockSpec((ROWS, PD), lambda i: (0, 0)),
        scratch_shapes=[
            pltpu.VMEM((2, words, examples), jnp.int32),
            pltpu.VMEM(narrow.shape, jnp.bfloat16),
            pltpu.SemaphoreType.DMA((2, blocks)),
            pltpu.SemaphoreType.DMA((blocks,)),
        ],
        input_output_aliases={2: 0},
        compiler_params=params(1),
        cost_estimate=cost(1e7),
        name="narrow_sum",
    )(hits, narrow, wide)


def swap(x, axis, size, bits):
    return lax.ppermute(x, axis, [(d, d ^ bits) for d in range(size)])


def local(sizes, grad_out, pooled, proj, assign, indices, lengths):
    count, slots, _ = grad_out.shape
    scale = 1.0 / math.sqrt(count * slots)
    n_node, n_local = sizes["node"], sizes["local"]
    n_plane = n_node // 2
    node, loc = lax.axis_index("node"), lax.axis_index("local")

    rows = proj[:, :W12]
    rows = jnp.concatenate([rows] + [swap(rows, "local", n_local, d) for d in range(1, n_local)])

    g12, g3, q = permute(assign, grad_out, pooled)

    rows, g3 = lax.optimization_barrier((rows, g3))
    rows = jnp.concatenate([rows] + [swap(rows, "node", n_node, 2 * d) for d in range(1, n_plane)])
    g3_got = lax.all_to_all(g3, AXES, split_axis=0, concat_axis=0, tiled=True)

    plane = jnp.arange(n_plane, dtype=jnp.int32) ^ (node // 2)
    lines = jnp.arange(n_local, dtype=jnp.int32) ^ loc
    (sent,) = partial_proj(plane * 2 + 1 - node % 2, lines, q, g12, g3, after=[rows])
    got = swap(sent, "node", n_node, 1)

    rows = jnp.concatenate([rows, swap(rows, "node", n_node, 1)])
    slot = jnp.arange(slots, dtype=jnp.int32)
    slot_node = slot // n_local ^ node
    slot_place = slot_node % 2 * (slots // 2) + slot_node // 2 * n_local + (slot % n_local ^ loc)
    narrow = narrow_dpool(slot_place, g12, rows)

    kept = partial_proj(plane * 2 + node % 2, lines, q, g12, g3, got, after=[narrow])
    arrived = [swap(kept[d], "node", n_node, 2 * d) for d in range(1, n_plane)]
    hits = count_hits(indices[0].transpose(1, 2, 0), lengths[0].T[:, None, :], after=kept[:1])

    narrow_sent, g3_got, hits = lax.optimization_barrier((narrow, g3_got, hits))
    narrow_got = lax.all_to_all(narrow_sent, AXES, split_axis=0, concat_axis=0, tiled=True)

    arrived, g3_got = lax.optimization_barrier((arrived, g3_got))
    total = kept[0]
    for term in arrived:
        total = total + term.astype(jnp.float32)
    own, terms = total[:1], [swap(total[d : d + 1], "local", n_local, d) for d in range(1, n_local)]

    wide = wide_sum(hits, g3_got.reshape(-1, PD), proj[0], after=[own])
    table_grad = narrow_sum(hits, narrow_got, wide)[None]
    terms, table_grad = lax.optimization_barrier((terms, table_grad))
    proj_grad = sum(terms, own) * scale
    return (table_grad, proj_grad)


def solution(mesh):
    placed = (
        P(AXES, None, None),
        P(AXES, None, None),
        P(AXES, None, None),
        P(),
        P(AXES, None, None, None),
        P(AXES, None, None),
    )
    return jax.shard_map(
        functools.partial(local, dict(mesh.shape)),
        mesh=mesh,
        in_specs=placed,
        out_specs=(P(AXES, None, None), P(AXES, None, None)),
        check_vma=False,
    )
```

time: 97.9 us -> 107 us (1.093)
  waiting for transfers between devices: 22.6 us -> 26.3 us
  Pallas kernels: 38.6 us -> 41.6 us
  local copies, waits for them, and re-layouts: 5.94 us -> 8.32 us
    ppermute x14, waiting for transfers between devices: 15.9 us -> 19.5 us  [swap(): return lax.ppermute(x, axis, [(d, d ^ bits) for d in range(size)])]
    pallas_call x5, Pallas kernels: 26.3 us -> 28.4 us  [the longest x2 8.84 us: partial_proj(): pl.pallas_call(functools.partial(partial_kernel, ins, len(after), len(sha...]
    unnamed x21 -> x25, local copies, waits for them, and re-layouts: 3.81 us -> 5.53 us
    pallas_call x1, Pallas kernels: 6.48 us -> 8.11 us  [permute(): pl.pallas_call(functools.partial(permute_kernel, slots, pieces), out_shap...]
  transfers between devices with their start and end apart: 16 -> 16, of which waited for: 7 -> 7; matrix products, arithmetic and copies ran while one was open for 5% -> 6% of each run, Pallas kernels for 29% -> 35%
where the time goes in v1:
time: 107 us; the launch traced here: 106 us
  Pallas kernels  41.6 us (39%)
  waiting for transfers between devices  26.3 us (25%)
  starting transfers between devices  26.2 us (24%)
  local copies, waits for them, and re-layouts  8.32 us (8%)
  other arithmetic  2.87 us (3%)
    ppermute x14, waiting for transfers between devices, swap(): return lax.ppermute(x, axis, [(d, d ^ bits) for d in range(size)])  19.5 us
    ppermute x14, starting transfers between devices, swap(): return lax.ppermute(x, axis, [(d, d ^ bits) for d in range(size)])  17.5 us
    pallas_call x2, Pallas kernels, partial_proj(): pl.pallas_call(functools.partial(partial_kernel, ins, len(after), len(sha...  8.84 us
    pallas_call x1, Pallas kernels, narrow_sum(): pl.pallas_call(functools.partial(narrow_sum_kernel, blocks), out_shape=ja...  8.28 us
    pallas_call x1, Pallas kernels, permute(): pl.pallas_call(functools.partial(permute_kernel, slots, pieces), out_shap...  8.11 us
    pallas_call x1, Pallas kernels, wide_sum(): pl.pallas_call(functools.partial(wide_kernel, blocks), out_shape=jax.Shap...  6.94 us
    all_to_all x1, waiting for transfers between devices, local(): g3_got = lax.all_to_all(g3, AXES, split_axis=0, concat_axis=0, tiled=True)  6.85 us
    unnamed x25, local copies, waits for them, and re-layouts  5.53 us
  transfers between devices with their start and end apart: 16, of which 7 were waited for; matrix products, arithmetic and copies ran while one was open for 6% of the time, Pallas kernels for 35%

profile of v1, /device:TPU:0, one launch (start us, length us, event | category | flops | bytes accessed | tf_op | source)
XLA Modules:
  0.0 106.2 jit_solution(12802393090820214880)
XLA Ops:
  0.6 0.7 slice.15
  1.4 3.0 %collective-permute-start = (bf16[1,64,128]{2,1,0:T(8,128)(2,1)S(1)}, bf16[1,64,128]{2,1,0:T(8,128)(2,1)S(1)}, u32[]{:S(2)}, u32[]{:S(2)}) collective-permute-start(bf16[1,64,128]{2,1,0:T(8,128)(2,1)S(1)} %slice.15), channel_id=1, source_target_pairs={{0,1},{1,0},{2,3},{3,2},{4,5},{5,4},{6,7},{7,6},{8,9},{9,8},{10,11... | collective-permute-start | bytes 49160 | tf_op jit(solution)/shard_map/ppermute | solution.py:363
  4.4 2.6 %collective-permute-start.1 = (bf16[1,64,128]{2,1,0:T(8,128)(2,1)S(1)}, bf16[1,64,128]{2,1,0:T(8,128)(2,1)S(1)}, u32[]{:S(2)}, u32[]{:S(2)}) collective-permute-start(bf16[1,64,128]{2,1,0:T(8,128)(2,1)S(1)} %slice.15), channel_id=1, source_target_pairs={{0,2},{1,3},{2,0},{3,1},{4,6},{5,7},{6,4},{7,5},{8,10},{9,11},{10,... | collective-permute-start | bytes 49160 | tf_op jit(solution)/shard_map/ppermute | solution.py:363
  8.0 8.1 %permute_groups.1 = (bf16[32,128,256]{2,1,0:T(8,128)(2,1)}, bf16[32,128,128]{2,1,0:T(8,128)(2,1)}, bf16[32,128,256]{2,1,0:T(8,128)(2,1)}) custom-call(s32[32]{0:T(128)} %assign_ref.1, bf16[128,32,384]{2,1,0:T(8,128)(2,1)} %grad_ref.1, bf16[128,32,256]{2,1,0:T(8,128)(2,1)} %pool_ref.1), custom_call_target="tpu_custom_call" | custom-call | flops 10000000 | bytes 1024 | tf_op jit(solution)/shard_map/permute_groups/pallas_call | solution.py:78
  16.2 1.8 %collective-permute-start.3 = (bf16[4,64,128]{2,1,0:T(8,128)(2,1)S(1)}, bf16[4,64,128]{2,1,0:T(8,128)(2,1)S(1)}, u32[]{:S(2)}, u32[]{:S(2)}) collective-permute-start(bf16[4,64,128]{2,1,0:T(8,128)(2,1)S(1)} %pad_maximum_fusion), channel_id=1, source_target_pairs={{0,8},{4,12},{8,0},{12,4},{16,24},{20,28},{24,16},{28,20},{1,9},{5... | collective-permute-start | bytes 196616 | tf_op jit(solution)/shard_map/ppermute | solution.py:363
  18.0 1.5 %collective-permute-start.4 = (bf16[4,64,128]{2,1,0:T(8,128)(2,1)S(1)}, bf16[4,64,128]{2,1,0:T(8,128)(2,1)S(1)}, u32[]{:S(2)}, u32[]{:S(2)}) collective-permute-start(bf16[4,64,128]{2,1,0:T(8,128)(2,1)S(1)} %pad_maximum_fusion), channel_id=1, source_target_pairs={{0,16},{4,20},{8,24},{12,28},{16,0},{20,4},{24,8},{28,12},{1,17},{... | collective-permute-start | bytes 196616 | tf_op jit(solution)/shard_map/ppermute | solution.py:363
  21.2 1.7 %collective-permute-done.4 = bf16[4,64,128]{2,1,0:T(8,128)(2,1)S(1)} collective-permute-done((bf16[4,64,128]{2,1,0:T(8,128)(2,1)S(1)}, bf16[4,64,128]{2,1,0:T(8,128)(2,1)S(1)}, u32[]{:S(2)}, u32[]{:S(2)}) %collective-permute-start.4) | collective-permute-done | bytes 65568 | tf_op jit(solution)/shard_map/ppermute | solution.py:363
  23.5 1.1 %collective-permute-done.5 = bf16[4,64,128]{2,1,0:T(8,128)(2,1)S(1)} collective-permute-done((bf16[4,64,128]{2,1,0:T(8,128)(2,1)S(1)}, bf16[4,64,128]{2,1,0:T(8,128)(2,1)S(1)}, u32[]{:S(2)}, u32[]{:S(2)}) %collective-permute-start.5) | collective-permute-done | bytes 65568 | tf_op jit(solution)/shard_map/ppermute | solution.py:363
  26.0 4.3 %partial_proj.2 = f32[16,256,128]{2,1,0:T(8,128)} custom-call(s32[4]{0:T(128)} %add_subtract_fusion.node_ref, s32[4]{0:T(128)} %iota_xor_fusion.line_ref, bf16[32,128,256]{2,1,0:T(8,128)(2,1)} %get-tuple-element.22.refs_0_, bf16[32,128,256]{2,1,0:T(8,128)(2,1)} %get-tuple-element.23.refs_1_.g_ref, bf16[32,128,128]{2,1,0:T(8,128)(2,1)} %get-tuple-element.25.refs_2_, ...), custom_call_target="tpu_custom_call" | custom-call | flops 10000000 | bytes 1024 | tf_op jit(solution)/shard_map/partial_proj/pallas_call | solution.py:205
  30.4 4.1 %all-to-all-start = ((bf16[32,128,128]{2,1,0:T(8,128)(2,1)}), bf16[32,128,128]{2,1,0:T(8,128)(2,1)S(1)}, u32[]{:S(2)}, u32[]{:S(2)}) async-start(bf16[32,128,128]{2,1,0:T(8,128)(2,1)} %get-tuple-element.25.refs_2_), calls=%async_computation | async-start | bytes 2097152 | tf_op jit(solution)/shard_map/all_to_all | solution.py:380
  37.3 4.4 %narrow_dpool.1.refs_4_ = bf16[32,64,128]{2,1,0:T(8,128)(2,1)} custom-call(s32[32]{0:T(128)} %fusion.1.place_ref, bf16[32,128,256]{2,1,0:T(8,128)(2,1)} %get-tuple-element.23.refs_1_.g_ref, bf16[32,64,128]{2,1,0:T(8,128)(2,1)} %constant_dynamic-update-slice_fusion.4.w_ref), custom_call_target="tpu_custom_call" | custom-call | flops 10000000 | bytes 1024 | tf_op jit(solution)/shard_map/narrow_dpool/pallas_call | solution.py:138
  41.6 1.4 %copy-done.2 = f32[16,256,128]{2,1,0:T(8,128)} copy-done((f32[16,256,128]{2,1,0:T(8,128)}, f32[16,256,128]{2,1,0:T(8,128)S(1)}, u32[]{:S(2)}) %copy-start.2) | copy-done | bytes 2097176
  43.0 4.5 %partial_proj.3 = (f32[4,256,128]{2,1,0:T(8,128)}, bf16[4,256,128]{2,1,0:T(8,128)(2,1)}, bf16[4,256,128]{2,1,0:T(8,128)(2,1)}, bf16[4,256,128]{2,1,0:T(8,128)(2,1)}) custom-call(s32[4]{0:T(128)} %fusion.5.node_ref, s32[4]{0:T(128)} %iota_xor_fusion.line_ref, bf16[32,128,256]{2,1,0:T(8,128)(2,1)} %get-tuple-element.22.refs_0_, ...), custom_call_target="tpu_custom_call" | custom-call | flops 10000000 | bytes 1024 | tf_op jit(solution)/shard_map/partial_proj/pallas_call | solution.py:205
  47.6 5.1 %count_hits.1.hits_ref = s32[3,64,4096]{2,1,0:T(8,128)} custom-call(s32[3,8,4096]{2,1,0:T(8,128)} %bitcast.13, s32[3,1,4096]{2,1,0:T(1,128)} %broadcast_in_dim.6.length_ref, f32[4,256,128]{2,1,0:T(8,128)} %get-tuple-element.27.refs_0_), custom_call_target="tpu_custom_call" | custom-call | flops 10000000 | bytes 1024 | tf_op jit(solution)/shard_map/count_hits/pallas_call | solution.py:249
  52.7 6.8 %all-to-all-done = bf16[32,128,128]{2,1,0:T(8,128)(2,1)S(1)} async-done(((bf16[32,128,128]{2,1,0:T(8,128)(2,1)}), bf16[32,128,128]{2,1,0:T(8,128)(2,1)S(1)}, u32[]{:S(2)}, u32[]{:S(2)}) %all-to-all-start) | async-done | bytes 1048608 | tf_op jit(solution)/shard_map/all_to_all | solution.py:380
  59.5 4.6 %all-to-all-start.1 = ((bf16[32,64,128]{2,1,0:T(8,128)(2,1)}), bf16[32,64,128]{2,1,0:T(8,128)(2,1)S(1)}, u32[]{:S(2)}, u32[]{:S(2)}) async-start(bf16[32,64,128]{2,1,0:T(8,128)(2,1)} %narrow_dpool.1.refs_4_), calls=%async_computation.1 | async-start | bytes 1048576 | tf_op jit(solution)/shard_map/all_to_all | solution.py:398
  64.2 2.6 %collective-permute-start.10 = (bf16[4,256,128]{2,1,0:T(8,128)(2,1)S(1)}, bf16[4,256,128]{2,1,0:T(8,128)(2,1)S(1)}, u32[]{:S(2)}, u32[]{:S(2)}) collective-permute-start(bf16[4,256,128]{2,1,0:T(8,128)(2,1)S(1)} %copy-done.9), channel_id=1, source_target_pairs={{0,24},{4,28},{8,16},{12,20},{16,8},{20,12},{24,0},{28,4},{1,25},{... | collective-permute-start | bytes 786440 | tf_op jit(solution)/shard_map/ppermute | solution.py:363
  67.7 11.9 %collective-permute-done.10 = bf16[4,256,128]{2,1,0:T(8,128)(2,1)S(1)} collective-permute-done((bf16[4,256,128]{2,1,0:T(8,128)(2,1)S(1)}, bf16[4,256,128]{2,1,0:T(8,128)(2,1)S(1)}, u32[]{:S(2)}, u32[]{:S(2)}) %collective-permute-start.10) | collective-permute-done | bytes 262176 | tf_op jit(solution)/shard_map/ppermute | solution.py:363
  79.6 4.4 %collective-permute-done.8 = bf16[4,256,128]{2,1,0:T(8,128)(2,1)S(1)} collective-permute-done((bf16[4,256,128]{2,1,0:T(8,128)(2,1)S(1)}, bf16[4,256,128]{2,1,0:T(8,128)(2,1)S(1)}, u32[]{:S(2)}, u32[]{:S(2)}) %collective-permute-start.8) | collective-permute-done | bytes 262176 | tf_op jit(solution)/shard_map/ppermute | solution.py:363
  85.1 1.8 %collective-permute-start.11 = (f32[1,256,128]{2,1,0:T(8,128)S(1)}, f32[1,256,128]{2,1,0:T(8,128)S(1)}, u32[]{:S(2)}, u32[]{:S(2)}) collective-permute-start(f32[1,256,128]{2,1,0:T(8,128)S(1)} %get-tuple-element.45), channel_id=1, source_target_pairs={{0,1},{1,0},{2,3},{3,2},{4,5},{5,4},{6,7},{7,6},{8,9},{9,8},{10,11... | collective-permute-start | bytes 393224 | tf_op jit(solution)/shard_map/ppermute | solution.py:363
  86.9 1.9 %collective-permute-start.12 = (f32[1,256,128]{2,1,0:T(8,128)S(1)}, f32[1,256,128]{2,1,0:T(8,128)S(1)}, u32[]{:S(2)}, u32[]{:S(2)}) collective-permute-start(f32[1,256,128]{2,1,0:T(8,128)S(1)} %get-tuple-element.44), channel_id=1, source_target_pairs={{0,2},{1,3},{2,0},{3,1},{4,6},{5,7},{6,4},{7,5},{8,10},{9,11},{10,... | collective-permute-start | bytes 393224 | tf_op jit(solution)/shard_map/ppermute | solution.py:363
  89.4 6.9 %wide_sum.1.wide_ref = f32[512,256]{1,0:T(8,128)} custom-call(s32[3,64,4096]{2,1,0:T(8,128)} %count_hits.1.hits_ref, bf16[4096,128]{1,0:T(8,128)(2,1)} %bitcast.11, bf16[256,128]{1,0:T(8,128)(2,1)} %bitcast.15, f32[1,256,128]{2,1,0:T(8,128)} %get-tuple-element.42.refs_0_), custom_call_target="tpu_custom_call" | custom-call | flops 10000000 | bytes 1024 | tf_op jit(solution)/shard_map/wide_sum/pallas_call | solution.py:302
  96.4 0.8 copy-done.1
  97.2 8.3 %narrow_sum.1 = f32[512,256]{1,0:T(8,128)} custom-call(s32[3,64,4096]{2,1,0:T(8,128)} %count_hits.1.hits_ref, bf16[32,64,128]{2,1,0:T(8,128)(2,1)} %copy-done.1, f32[512,256]{1,0:T(8,128)} %wide_sum.1.wide_ref), custom_call_target="tpu_custom_call", output_to_operand_aliasing={{}: (2, {})} | custom-call | flops 10000000 | bytes 1024 | tf_op jit(solution)/shard_map/narrow_sum/pallas_call | solution.py:343
  (51 shorter events, 11.0 us)
Async XLA Ops:
  1.4 14.8 %collective-permute-start = (bf16[1,64,128]{2,1,0:T(8,128)(2,1)S(1)}, bf16[1,64,128]{2,1,0:T(8,128)(2,1)S(1)}, u32[]{:S(2)}, u32[]{:S(2)}) collective-permute-start(bf16[1,64,128]{2,1,0:T(8,128)(2,1)S(1)} %slice.15), channel_id=1, source_target_pairs={{0,1},{1,0},{2,3},{3,2},{4,5},{5,4},{6,7},{7,6},{8,9},{9,8},{10,11... | collective-permute-start | bytes 49160 | tf_op jit(solution)/shard_map/ppermute | solution.py:363
  4.4 11.8 %collective-permute-start.1 = (bf16[1,64,128]{2,1,0:T(8,128)(2,1)S(1)}, bf16[1,64,128]{2,1,0:T(8,128)(2,1)S(1)}, u32[]{:S(2)}, u32[]{:S(2)}) collective-permute-start(bf16[1,64,128]{2,1,0:T(8,128)(2,1)S(1)} %slice.15), channel_id=1, source_target_pairs={{0,2},{1,3},{2,0},{3,1},{4,6},{5,7},{6,4},{7,5},{8,10},{9,11},{10,... | collective-permute-start | bytes 49160 | tf_op jit(solution)/shard_map/ppermute | solution.py:363
  7.0 9.2 %collective-permute-start.2 = (bf16[1,64,128]{2,1,0:T(8,128)(2,1)S(1)}, bf16[1,64,128]{2,1,0:T(8,128)(2,1)S(1)}, u32[]{:S(2)}, u32[]{:S(2)}) collective-permute-start(bf16[1,64,128]{2,1,0:T(8,128)(2,1)S(1)} %slice.15), channel_id=1, source_target_pairs={{0,3},{1,2},{2,1},{3,0},{4,7},{5,6},{6,5},{7,4},{8,11},{9,10},{10,... | collective-permute-start | bytes 49160 | tf_op jit(solution)/shard_map/ppermute | solution.py:363
  16.2 4.3 %collective-permute-start.3 = (bf16[4,64,128]{2,1,0:T(8,128)(2,1)S(1)}, bf16[4,64,128]{2,1,0:T(8,128)(2,1)S(1)}, u32[]{:S(2)}, u32[]{:S(2)}) collective-permute-start(bf16[4,64,128]{2,1,0:T(8,128)(2,1)S(1)} %pad_maximum_fusion), channel_id=1, source_target_pairs={{0,8},{4,12},{8,0},{12,4},{16,24},{20,28},{24,16},{28,20},{1,9},{5... | collective-permute-start | bytes 196616 | tf_op jit(solution)/shard_map/ppermute | solution.py:363
  18.0 4.9 %collective-permute-start.4 = (bf16[4,64,128]{2,1,0:T(8,128)(2,1)S(1)}, bf16[4,64,128]{2,1,0:T(8,128)(2,1)S(1)}, u32[]{:S(2)}, u32[]{:S(2)}) collective-permute-start(bf16[4,64,128]{2,1,0:T(8,128)(2,1)S(1)} %pad_maximum_fusion), channel_id=1, source_target_pairs={{0,16},{4,20},{8,24},{12,28},{16,0},{20,4},{24,8},{28,12},{1,17},{... | collective-permute-start | bytes 196616 | tf_op jit(solution)/shard_map/ppermute | solution.py:363
  19.5 5.2 %collective-permute-start.5 = (bf16[4,64,128]{2,1,0:T(8,128)(2,1)S(1)}, bf16[4,64,128]{2,1,0:T(8,128)(2,1)S(1)}, u32[]{:S(2)}, u32[]{:S(2)}) collective-permute-start(bf16[4,64,128]{2,1,0:T(8,128)(2,1)S(1)} %pad_maximum_fusion), channel_id=1, source_target_pairs={{0,24},{4,28},{8,16},{12,20},{16,8},{20,12},{24,0},{28,4},{1,25},{... | collective-permute-start | bytes 196616 | tf_op jit(solution)/shard_map/ppermute | solution.py:363
  30.3 4.2 %copy-start.5 = (bf16[16,64,128]{2,1,0:T(8,128)(2,1)S(1)}, bf16[16,64,128]{2,1,0:T(8,128)(2,1)}, u32[]{:S(2)}) copy-start(bf16[16,64,128]{2,1,0:T(8,128)(2,1)} %copy-done.4) | copy-start | bytes 786436
  30.3 4.5 %copy-start.6 = (s32[1,4096,3]{1,0,2:T(1,128)S(1)}, s32[1,4096,3]{1,0,2:T(1,128)}, u32[]{:S(2)}) copy-start(s32[1,4096,3]{1,0,2:T(1,128)} %param.11) | copy-start | bytes 147460
  30.3 11.3 %collective-permute-start.6 = (f32[16,256,128]{2,1,0:T(8,128)}, f32[16,256,128]{2,1,0:T(8,128)S(1)}, u32[]{:S(2)}, u32[]{:S(2)}) collective-permute-start(f32[16,256,128]{2,1,0:T(8,128)} %partial_proj.2), channel_id=1, source_target_pairs={{0,4},{4,0},{8,12},{12,8},{16,20},{20,16},{24,28},{28,24},{1,5},{5... | collective-permute-start | bytes 6291464 | tf_op jit(solution)/shard_map/ppermute | solution.py:363
  30.4 29.1 %all-to-all-start = ((bf16[32,128,128]{2,1,0:T(8,128)(2,1)}), bf16[32,128,128]{2,1,0:T(8,128)(2,1)S(1)}, u32[]{:S(2)}, u32[]{:S(2)}) async-start(bf16[32,128,128]{2,1,0:T(8,128)(2,1)} %get-tuple-element.25.refs_2_), calls=%async_computation | async-start | bytes 2097152 | tf_op jit(solution)/shard_map/all_to_all | solution.py:380
  34.5 2.1 %collective-permute-start.7 = (bf16[16,64,128]{2,1,0:T(8,128)(2,1)S(1)}, bf16[16,64,128]{2,1,0:T(8,128)(2,1)S(1)}, u32[]{:S(2)}, u32[]{:S(2)}) collective-permute-start(bf16[16,64,128]{2,1,0:T(8,128)(2,1)S(1)} %copy-done.5), channel_id=1, source_target_pairs={{0,4},{4,0},{8,12},{12,8},{16,20},{20,16},{24,28},{28,24},{1,5},{5... | collective-permute-start | bytes 786440 | tf_op jit(solution)/shard_map/ppermute | solution.py:363
  41.6 1.4 %copy-start.2 = (f32[16,256,128]{2,1,0:T(8,128)}, f32[16,256,128]{2,1,0:T(8,128)S(1)}, u32[]{:S(2)}) copy-start(f32[16,256,128]{2,1,0:T(8,128)S(1)} %collective-permute-done.6.refs_3_) | copy-start | bytes 6291460
  47.6 16.6 %copy-start.9 = (bf16[4,256,128]{2,1,0:T(8,128)(2,1)S(1)}, bf16[4,256,128]{2,1,0:T(8,128)(2,1)}, u32[]{:S(2)}) copy-start(bf16[4,256,128]{2,1,0:T(8,128)(2,1)} %get-tuple-element.30) | copy-start | bytes 786436
  47.6 19.2 %copy-start.8 = (bf16[4,256,128]{2,1,0:T(8,128)(2,1)S(1)}, bf16[4,256,128]{2,1,0:T(8,128)(2,1)}, u32[]{:S(2)}) copy-start(bf16[4,256,128]{2,1,0:T(8,128)(2,1)} %get-tuple-element.28) | copy-start | bytes 786436
  47.6 19.7 %copy-start.7 = (bf16[4,256,128]{2,1,0:T(8,128)(2,1)S(1)}, bf16[4,256,128]{2,1,0:T(8,128)(2,1)}, u32[]{:S(2)}) copy-start(bf16[4,256,128]{2,1,0:T(8,128)(2,1)} %get-tuple-element.29) | copy-start | bytes 786436
  47.6 36.7 %copy-start.3 = (f32[4,256,128]{2,1,0:T(8,128)S(1)}, f32[4,256,128]{2,1,0:T(8,128)}, u32[]{:S(2)}) copy-start(f32[4,256,128]{2,1,0:T(8,128)} %get-tuple-element.27.refs_0_) | copy-start | bytes 1572868
  59.5 29.9 %copy-start = (bf16[32,128,128]{2,1,0:T(8,128)(2,1)}, bf16[32,128,128]{2,1,0:T(8,128)(2,1)S(1)}, u32[]{:S(2)}) copy-start(bf16[32,128,128]{2,1,0:T(8,128)(2,1)S(1)} %all-to-all-done) | copy-start | bytes 3145732
  59.5 36.9 %all-to-all-start.1 = ((bf16[32,64,128]{2,1,0:T(8,128)(2,1)}), bf16[32,64,128]{2,1,0:T(8,128)(2,1)S(1)}, u32[]{:S(2)}, u32[]{:S(2)}) async-start(bf16[32,64,128]{2,1,0:T(8,128)(2,1)} %narrow_dpool.1.refs_4_), calls=%async_computation.1 | async-start | bytes 1048576 | tf_op jit(solution)/shard_map/all_to_all | solution.py:398
  64.2 15.4 %collective-permute-start.10 = (bf16[4,256,128]{2,1,0:T(8,128)(2,1)S(1)}, bf16[4,256,128]{2,1,0:T(8,128)(2,1)S(1)}, u32[]{:S(2)}, u32[]{:S(2)}) collective-permute-start(bf16[4,256,128]{2,1,0:T(8,128)(2,1)S(1)} %copy-done.9), channel_id=1, source_target_pairs={{0,24},{4,28},{8,16},{12,20},{16,8},{20,12},{24,0},{28,4},{1,25},{... | collective-permute-start | bytes 786440 | tf_op jit(solution)/shard_map/ppermute | solution.py:363
  66.7 17.3 %collective-permute-start.8 = (bf16[4,256,128]{2,1,0:T(8,128)(2,1)S(1)}, bf16[4,256,128]{2,1,0:T(8,128)(2,1)S(1)}, u32[]{:S(2)}, u32[]{:S(2)}) collective-permute-start(bf16[4,256,128]{2,1,0:T(8,128)(2,1)S(1)} %copy-done.8), channel_id=1, source_target_pairs={{0,8},{4,12},{8,0},{12,4},{16,24},{20,28},{24,16},{28,20},{1,9},{5... | collective-permute-start | bytes 786440 | tf_op jit(solution)/shard_map/ppermute | solution.py:363
  67.3 16.9 %collective-permute-start.9 = (bf16[4,256,128]{2,1,0:T(8,128)(2,1)S(1)}, bf16[4,256,128]{2,1,0:T(8,128)(2,1)S(1)}, u32[]{:S(2)}, u32[]{:S(2)}) collective-permute-start(bf16[4,256,128]{2,1,0:T(8,128)(2,1)S(1)} %copy-done.7), channel_id=1, source_target_pairs={{0,16},{4,20},{8,24},{12,28},{16,0},{20,4},{24,8},{28,12},{1,17},{... | collective-permute-start | bytes 786440 | tf_op jit(solution)/shard_map/ppermute | solution.py:363
  85.1 20.4 %collective-permute-start.11 = (f32[1,256,128]{2,1,0:T(8,128)S(1)}, f32[1,256,128]{2,1,0:T(8,128)S(1)}, u32[]{:S(2)}, u32[]{:S(2)}) collective-permute-start(f32[1,256,128]{2,1,0:T(8,128)S(1)} %get-tuple-element.45), channel_id=1, source_target_pairs={{0,1},{1,0},{2,3},{3,2},{4,5},{5,4},{6,7},{7,6},{8,9},{9,8},{10,11... | collective-permute-start | bytes 393224 | tf_op jit(solution)/shard_map/ppermute | solution.py:363
  86.9 18.6 %collective-permute-start.12 = (f32[1,256,128]{2,1,0:T(8,128)S(1)}, f32[1,256,128]{2,1,0:T(8,128)S(1)}, u32[]{:S(2)}, u32[]{:S(2)}) collective-permute-start(f32[1,256,128]{2,1,0:T(8,128)S(1)} %get-tuple-element.44), channel_id=1, source_target_pairs={{0,2},{1,3},{2,0},{3,1},{4,6},{5,7},{6,4},{7,5},{8,10},{9,11},{10,... | collective-permute-start | bytes 393224 | tf_op jit(solution)/shard_map/ppermute | solution.py:363
  88.8 16.7 %collective-permute-start.13 = (f32[1,256,128]{2,1,0:T(8,128)S(1)}, f32[1,256,128]{2,1,0:T(8,128)S(1)}, u32[]{:S(2)}, u32[]{:S(2)}) collective-permute-start(f32[1,256,128]{2,1,0:T(8,128)S(1)} %get-tuple-element.43), channel_id=1, source_target_pairs={{0,3},{1,2},{2,1},{3,0},{4,7},{5,6},{6,5},{7,4},{8,11},{9,10},{10,... | collective-permute-start | bytes 393224 | tf_op jit(solution)/shard_map/ppermute | solution.py:363
  (2 other events, 1.5 us)
